TPU v7x, 32 devices: a whole 2x2x4 slice. The times are simulated.
32 devices in a mesh: group: 4 (over y, core), vocab: 8 (over z, x).
Axes of the slice: x: 2, y: 2, z: 4, core: 2. Of those that a mesh axis runs over, the one named last changes fastest.
Arguments:
- hidden: bfloat16 [16, 2560], P('group', 'vocab'), as said below
- dealt_slot: int32 [16], P('group'), may hold values from 0 to 15, as said below
- targets: int32 [16], P('group'), may hold values from 0 to 16383
- final_gain: float32 [2560], replicated, may hold values from 0.5 to 1.5
- vocab_head: bfloat16 [16384, 2560], P(('group', 'vocab')), as said below
- first_gain: float32 [2560], replicated, may hold values from 0.25 to 1.75
- qkv_weight: bfloat16 [2560, 3072], P(None, 'vocab'), may hold values from -0.125 to 0.125
Outputs:
- logprob: float32 [16], P('group')
- entropy: float32 [16], P('group')
- qkv_out: bfloat16 [3072, 16], P('vocab', 'group')
Inputs may be any that keep to these rules, and one draw needn't show every extreme that they name: dealt_slot is a permutation of the 16 slots; position r is owned by group r // 4, slot s belongs to group s // 4, and the positions owned by each group go exactly 1 to every group. `vocab_head`: independent rows, none zero. `hidden`: independent rows, none zero.
All inputs are finite; a program needn't handle non-finite values.
Results may differ from a plain program's by a relative error of at most 0.001.
The roundings to bfloat16 on the way count: a program that leaves them out, or rounds other values in their place, can miss the bound.
Values may be sent and summed in bfloat16 or wider, within the bound.
A program may use at most 64 MiB of HBM per device.

v0:
```python
import jax
import jax.numpy as jnp
from jax import lax
from jax.sharding import PartitionSpec as P

eps = 1e-06


def joined(array, axis, combine):
    everything = jax.tree.map(lambda part: lax.all_gather(part, axis), array)
    leading = jax.tree.map(lambda part: part[0], everything)

    def step(k, so_far):
        return combine(so_far, jax.tree.map(lambda part: part[k], everything))

    return lax.fori_loop(1, lax.axis_size(axis), step, leading)


def rms_scaled(values, gain):
    wide = values.astype(jnp.float32)
    factor = lax.rsqrt(jnp.mean(wide * wide, axis=-1, keepdims=True) + eps)
    return (wide * factor * gain).astype(jnp.bfloat16)


def merge_stats(earlier, later):
    first_top, first_total, first_weighted, first_target = earlier
    second_top, second_total, second_weighted, second_target = later
    joint_top = jnp.maximum(first_top, second_top)
    first_scale = jnp.exp(first_top - joint_top)
    second_scale = jnp.exp(second_top - joint_top)
    joint_total = first_total * first_scale + second_total * second_scale
    joint_weighted = first_scale * (
        first_weighted + first_total * (first_top - joint_top)
    ) + second_scale * (second_weighted + second_total * (second_top - joint_top))
    return (joint_top, joint_total, joint_weighted, first_target + second_target)


def local(hidden, dealt_slot, targets, final_gain, vocab_head, first_gain, qkv_weight):
    groups = lax.axis_size("group")
    shards = lax.axis_size("vocab")
    row_group = hidden.shape[0]
    col_count = hidden.shape[1]
    quota = row_group // groups
    rows_all = row_group * groups
    vocab_dev = vocab_head.shape[0]
    row_iota = jnp.arange(row_group, dtype=jnp.int32)
    dest_group = dealt_slot // row_group
    group_hits = (dest_group[:, None] == jnp.arange(groups, dtype=jnp.int32)[None, :]).astype(
        jnp.int32
    )
    earlier_hits = jnp.cumsum(group_hits, axis=0) - group_hits
    send_rank = jnp.sum(earlier_hits * group_hits, axis=1)
    position = dest_group * quota + send_rank
    packer = position[None, :] == row_iota[:, None]
    send_rows = jnp.dot(packer.astype(jnp.float32), hidden.astype(jnp.float32)).astype(jnp.bfloat16)
    send_slots = jnp.sum(jnp.where(packer, dealt_slot[None, :], 0), axis=1)
    send_targets = jnp.sum(jnp.where(packer, targets[None, :], 0), axis=1)
    arrived, arrived_slots, arrived_targets = (
        lax.all_to_all(
            send_rows.reshape(groups, quota, col_count),
            "group",
            split_axis=0,
            concat_axis=0,
            tiled=True,
        ),
        lax.all_to_all(
            send_slots.reshape(groups, quota), "group", split_axis=0, concat_axis=0, tiled=True
        ),
        lax.all_to_all(
            send_targets.reshape(groups, quota), "group", split_axis=0, concat_axis=0, tiled=True
        ),
    )
    arrived = arrived.reshape(row_group, col_count)
    local_slot = arrived_slots.reshape(row_group) % row_group
    placer = local_slot[None, :] == row_iota[:, None]
    dealt_cols = jnp.dot(placer.astype(jnp.float32), arrived.astype(jnp.float32)).astype(
        jnp.bfloat16
    )
    dealt_targets = jnp.sum(
        jnp.where(placer, arrived_targets.reshape(row_group)[None, :], 0), axis=1
    )
    dealt_rows = lax.all_gather(dealt_cols, "vocab", axis=1, tiled=True)
    normed = rms_scaled(dealt_rows, final_gain)
    offset = (lax.axis_index("group") * shards + lax.axis_index("vocab")) * vocab_dev
    vocab_iota = jnp.arange(vocab_dev, dtype=jnp.int32)
    head_wide = vocab_head.astype(jnp.float32)
    wanted_all = jnp.zeros((rows_all,), jnp.int32)
    rows_piece = lax.all_gather(normed, "group", axis=0, tiled=True)
    wanted = lax.all_gather(dealt_targets, "group", axis=0, tiled=True)
    logits = jnp.einsum("rd,vd->rv", rows_piece.astype(jnp.float32), head_wide)
    matches = (wanted - offset)[:, None] == vocab_iota[None, :]
    target_logit = jnp.sum(jnp.where(matches, logits, 0.0), axis=1)
    shard_top = jnp.max(logits, axis=1)
    shifted = logits - shard_top[:, None]
    expons = jnp.exp(shifted)
    shard_total = jnp.sum(expons, axis=1)
    shard_weighted = jnp.sum(expons * shifted, axis=1)
    shard_top, shard_total, shard_weighted, target_logit, all_targets = (
        shard_top,
        shard_total,
        shard_weighted,
        target_logit,
        lax.dynamic_update_slice_in_dim(wanted_all, wanted, jnp.int32(0), 0),
    )
    row_top, row_total, row_weighted, row_target = joined(
        (shard_top, shard_total, shard_weighted, target_logit), ("group", "vocab"), merge_stats
    )
    log_total = jnp.log(row_total)
    slot_logprob = row_target - row_top - log_total
    slot_entropy = log_total - row_weighted / row_total
    logprob = jnp.take(slot_logprob, dealt_slot, axis=0)
    entropy = jnp.take(slot_entropy, dealt_slot, axis=0)
    local_ids = all_targets - offset
    inside = (local_ids >= 0) & (local_ids < vocab_dev)
    picked_rows = jnp.take(vocab_head, jnp.clip(local_ids, 0, vocab_dev - 1), axis=0)
    partial_rows = jnp.where(inside[:, None], picked_rows, jnp.zeros_like(picked_rows))
    shared = lax.psum_scatter(
        partial_rows.astype(jnp.float32).astype(jnp.bfloat16),
        "group",
        scatter_dimension=0,
        tiled=True,
    )
    weight_wide = qkv_weight.astype(jnp.float32)
    embedded = lax.psum(shared, "vocab").astype(jnp.float32)
    first_normed = rms_scaled(embedded, first_gain)
    projected = jnp.einsum("rd,dc->cr", first_normed.astype(jnp.float32), weight_wide)
    return (logprob, entropy, projected.astype(jnp.bfloat16))


def solution(mesh):
    return jax.shard_map(
        local,
        mesh=mesh,
        in_specs=(
            P("group", "vocab"),
            P("group"),
            P("group"),
            P(),
            P(("group", "vocab"), None),
            P(),
            P(None, "vocab"),
        ),
        out_specs=(P("group"), P("group"), P("vocab", "group")),
        check_vma=False,
    )
```

profile of v0, /device:TPU:0, one launch (start us, length us, event | category | flops | bytes accessed | tf_op | source)
XLA Modules:
  0.0 167.4 jit_solution(10437662355983042251)
XLA Ops:
  7.2 0.8 compare_select_fusion.6
  8.0 0.1 fusion.23
  8.1 0.2 select_reduce_fusion.4
  8.3 0.8 select_reduce_fusion.2
  9.1 0.7 copy.23
  9.8 4.2 %all-to-all-start = ((s32[4,1,1]{2,1,0:T(1,128)}), s32[4,1,1]{2,1,0:T(1,128)S(1)}, u32[]{:S(2)}, u32[]{:S(2)}) async-start(s32[4,1,1]{2,1,0:T(1,128)} %copy.23), calls=%async_computation | async-start | bytes 4096 | tf_op jit(solution)/shard_map/all_to_all | solution.py:66
  14.0 0.8 fusion.11
  14.8 0.5 broadcast.188
  15.3 0.7 reduce.3
  16.0 0.7 reshape.149
  16.7 0.7 copy.26
  17.4 1.3 fusion.28
  20.0 3.3 %all-to-all-start.2 = ((s32[4,1,1]{2,1,0:T(1,128)}), s32[4,1,1]{2,1,0:T(1,128)S(1)}, u32[]{:S(2)}, u32[]{:S(2)}) async-start(s32[4,1,1]{2,1,0:T(1,128)} %copy.26), calls=%async_computation.2 | async-start | bytes 4096 | tf_op jit(solution)/shard_map/all_to_all | solution.py:69
  23.3 0.2 reduce.1
  23.5 3.6 %all-to-all-done.2 = s32[4,1,1]{2,1,0:T(1,128)S(1)} async-done(((s32[4,1,1]{2,1,0:T(1,128)}), s32[4,1,1]{2,1,0:T(1,128)S(1)}, u32[]{:S(2)}, u32[]{:S(2)}) %all-to-all-start.2) | async-done | bytes 48 | tf_op jit(solution)/shard_map/all_to_all | solution.py:69
  27.1 3.2 %all-to-all-start.1 = ((bf16[4,2,160]{2,1,0:T(2,128)(2,1)}), bf16[4,2,160]{2,1,0:T(2,128)(2,1)S(1)}, u32[]{:S(2)}, u32[]{:S(2)}) async-start(bf16[4,2,160]{2,1,0:T(2,128)(2,1)} %reshape.149), calls=%async_computation.1 | async-start | bytes 8192 | tf_op jit(solution)/shard_map/all_to_all | solution.py:59
  30.4 0.2 reduce.2
  30.5 0.1 select_reduce_fusion.1
  30.6 0.2 dynamic-update-slice.3
  30.9 5.4 %all-reduce.3 = s32[16]{0:T(128)S(1)} all-reduce(s32[16]{0:T(128)S(1)} %dynamic-update-slice.3), channel_id=1, replica_groups=mesh['group'=4,'vocab'=8] {'group'}, use_global_device_ids=true, to_apply=%add.3 | all-reduce | flops 16 | bytes 128
  36.3 0.6 gather_fusion
  36.9 0.7 select_select_fusion
  37.6 0.1 reshape.150
  37.7 0.1 fusion.12
  37.9 31.1 %all-gather.4 = bf16[8,320,4]{1,2,0:T(4,128)(2,1)S(1)} all-gather(bf16[1,320,4]{1,2,0:T(4,128)(2,1)S(1)} %fusion.12), channel_id=1, replica_groups=mesh['group'=4,'vocab'=8] {'vocab'}, dimensions={0}, use_global_device_ids=true | all-gather | bytes 23040 | tf_op jit(solution)/shard_map/all_gather | solution.py:82
  68.9 0.1 reshape.141
  69.0 0.1 multiply_reduce_fusion
  69.2 0.8 fusion.17
  70.0 5.3 %all-gather.5 = bf16[4,4,2560]{2,1,0:T(4,128)(2,1)S(1)} all-gather(bf16[1,4,2560]{2,1,0:T(4,128)(2,1)S(1)} %fusion.17), channel_id=1, replica_groups=mesh['group'=4,'vocab'=8] {'group'}, dimensions={0}, use_global_device_ids=true | all-gather | bytes 102400 | tf_op jit(solution)/shard_map/all_gather | solution.py:88
  75.3 0.9 fusion.29
  76.2 0.2 fusion.16
  76.4 0.2 dynamic-update-slice
  76.7 0.2 dynamic-update-slice.1
  76.9 0.2 dynamic-update-slice.2
  77.1 0.2 dynamic-update-slice.4
  77.3 38.9 %all-reduce.6 = (f32[512]{0:T(512)S(1)}, f32[512]{0:T(512)S(1)}, f32[512]{0:T(512)S(1)}, f32[512]{0:T(512)S(1)}) all-reduce(f32[512]{0:T(512)S(1)} %dynamic-update-slice, f32[512]{0:T(512)S(1)} %dynamic-update-slice.1, f32[512]{0:T(512)S(1)} %dynamic-update-slice.2, ...), channel_id=2, replica_groups=mesh['group'=4,'vocab'=8] {'group','vocab'}, use_global_device_ids=true, to_apply=%add | all-reduce | flops 2048 | bytes 16384
  116.2 0.1 reshape.109
  116.2 0.1 reshape.110
  116.3 0.1 reshape.111
  116.4 0.1 reshape.112
  116.5 2.7 %while.21 = (s32[]{:T(128)}, f32[16]{0:T(128)S(1)}, f32[16]{0:T(128)S(1)}, f32[16]{0:T(128)S(1)}, f32[16]{0:T(128)S(1)}, /*index=5*/f32[32,16]{1,0:T(8,128)S(1)}...) while((s32[]{:T(128)}, f32[16]{0:T(128)S(1)}, ...), condition=%wide.region_11.12_spmd, body=%wide.region_10.11_spmd.sunk | while | flops 261 | bytes 1383 | solution.py:16
  119.2 0.6 gather_fusion.2
  119.8 0.6 gather_fusion.1
  120.5 0.5 broadcast_select_fusion
  121.0 0.8 constant_dynamic-slice_fusion.4
  121.8 36.1 %psum.7 = bf16[4,2560]{1,0:T(4,128)(2,1)S(1)} all-reduce(bf16[4,2560]{1,0:T(4,128)(2,1)S(1)} %constant_dynamic-slice_fusion.4), channel_id=1, replica_groups=mesh['group'=4,'vocab'=8] {'vocab'}, use_global_device_ids=true, to_apply=%region_13.15 | all-reduce | flops 10240 | bytes 40960 | tf_op jit(solution)/shard_map/psum | solution.py:124
  157.9 0.1 fusion.13
  158.0 2.5 %fusion.10 = bf16[384,4]{0,1:T(4,128)(2,1)} fusion(bf16[2560,384]{1,0:T(8,128)(2,1)} %param.17, bf16[4,2560]{1,0:T(4,128)(2,1)S(1)} %psum.7, f32[2560]{0:T(1024)S(1)} %copy-done.1, f32[4]{0:T(128)S(1)} %add_rsqrt_fusion), kind=kOutput, calls=%fused_computation.21 | convolution fusion | flops 7906816 | bytes 1999888 | tf_op jit(solution)/shard_map/rd,dc->cr/dot_general | solution.py:126
  (125 shorter events, 2.0 us)
Async XLA Ops:
  7.2 29.1 %copy-start = (bf16[512,2560]{1,0:T(8,128)(2,1)S(1)}, bf16[512,2560]{1,0:T(8,128)(2,1)}, u32[]{:S(2)}) copy-start(bf16[512,2560]{1,0:T(8,128)(2,1)} %param.15) | copy-start | bytes 7864324
  9.8 10.2 %all-to-all-start = ((s32[4,1,1]{2,1,0:T(1,128)}), s32[4,1,1]{2,1,0:T(1,128)S(1)}, u32[]{:S(2)}, u32[]{:S(2)}) async-start(s32[4,1,1]{2,1,0:T(1,128)} %copy.23), calls=%async_computation | async-start | bytes 4096 | tf_op jit(solution)/shard_map/all_to_all | solution.py:66
  20.0 7.1 %all-to-all-start.2 = ((s32[4,1,1]{2,1,0:T(1,128)}), s32[4,1,1]{2,1,0:T(1,128)S(1)}, u32[]{:S(2)}, u32[]{:S(2)}) async-start(s32[4,1,1]{2,1,0:T(1,128)} %copy.26), calls=%async_computation.2 | async-start | bytes 4096 | tf_op jit(solution)/shard_map/all_to_all | solution.py:69
  27.1 10.6 %all-to-all-start.1 = ((bf16[4,2,160]{2,1,0:T(2,128)(2,1)}), bf16[4,2,160]{2,1,0:T(2,128)(2,1)S(1)}, u32[]{:S(2)}, u32[]{:S(2)}) async-start(bf16[4,2,160]{2,1,0:T(2,128)(2,1)} %reshape.149), calls=%async_computation.1 | async-start | bytes 8192 | tf_op jit(solution)/shard_map/all_to_all | solution.py:59
  30.3 90.7 %all-reduce.9.cloned.1.call-start = ((), (), s32[]{:S(2)}) async-start(), calls=%async_computation.3 | async-start | bytes 163840
  36.9 83.6 %copy-start.2 = (s32[4]{0:T(128)S(1)}, s32[4]{0:T(128)}, u32[]{:S(2)}) copy-start(s32[4]{0:T(128)} %param.12) | copy-start | bytes 52
  36.9 121.1 %copy-start.1 = (f32[2560]{0:T(1024)S(1)}, f32[2560]{0:T(1024)}, u32[]{:S(2)}) copy-start(f32[2560]{0:T(1024)} %param.16) | copy-start | bytes 30724
Sparse Core Ops, SparseCore 0:
  37.8 30.6 all-reduce.8
where the time goes:
time: 168 us; the launch traced here: 167 us
  blocking collectives  117 us (70%)
  between operations  15.5 us (9%)
  starting transfers between devices  10.8 us (6%)
  local copies, waits for them, and re-layouts  8.28 us (5%)
  other arithmetic  7.31 us (4%)
  matrix products  4.37 us (3%)
  waiting for transfers between devices  3.6 us (2%)
    unnamed x2, blocking collectives  44.2 us
    psum x1, blocking collectives, local(): embedded = lax.psum(shared, 'vocab').astype(jnp.float32)  36.1 us
    all_gather x1, blocking collectives, local(): dealt_rows = lax.all_gather(dealt_cols, 'vocab', axis=1, tiled=True)  31.1 us
    all_gather x1, blocking collectives, local(): rows_piece = lax.all_gather(normed, 'group', axis=0, tiled=True)  5.29 us
    all_to_all x1, starting transfers between devices, local(): lax.all_to_all(send_slots.reshape(groups, quota), 'group', split_axis=0,...  4.24 us
    unnamed x21, local copies, waits for them, and re-layouts  4.04 us
    all_to_all x1, waiting for transfers between devices, local(): lax.all_to_all(send_targets.reshape(groups, quota), 'group', split_axis=0...  3.58 us
  transfers between devices with their start and end apart: 4, of which 1 were waited for; matrix products, arithmetic and copies ran while one was open for 8% of the time, Pallas kernels for 0%

commit v1 on v0

v1 whole, which is shorter than its diff:
```python
import functools

import jax
import jax.numpy as jnp
from jax import lax
from jax.experimental import pallas as pl
from jax.experimental.pallas import tpu as pltpu
from jax.sharding import PartitionSpec as P

eps = 1e-06
MESH = pl.DeviceIdType.MESH
LANES = 128
UNROLL_MAX = 32


def each(first, last, body):
    if last - first <= UNROLL_MAX:
        for k in range(first, last):
            body(k)
    else:

        def step(k, carry):
            body(k)
            return carry

        lax.fori_loop(first, last, step, 0)


def rms_scaled(wide, gain):
    factor = lax.rsqrt(jnp.mean(wide * wide, axis=-1, keepdims=True) + eps)
    return (wide * factor * gain).astype(jnp.bfloat16)


def merged(ref):
    tops = ref[:, 0:1, :]
    totals = ref[:, 1:2, :]
    top = jnp.max(tops, axis=0, keepdims=True)
    gap = tops - top
    scale = jnp.exp(gap)
    total = jnp.sum(scale * totals, axis=0)
    weighted = jnp.sum(scale * (ref[:, 2:3, :] + totals * gap), axis=0)
    target = jnp.sum(ref[:, 3:4, :], axis=0)
    return top[0], total, weighted, target


def put_stats(ref, k, stats):
    for row, stat in enumerate(stats):
        ref[k, row : row + 1, :] = stat


def kernel(
    groups,
    shards,
    starts,
    width,
    hidden_ref,
    slot_ref,
    target_ref,
    final_gain_ref,
    head_hbm,
    first_gain_ref,
    qkv_hbm,
    logprob_ref,
    entropy_ref,
    out_ref,
    head,
    qkv,
    ids,
    pieces,
    wide_rows,
    normed,
    rows_all,
    picked,
    picked_out,
    picked_in,
    summed,
    embedded,
    stats_one,
    stats_two,
    local_sem,
    send_sem,
    recv_sem,
):
    group = lax.axis_index("group")
    shard = lax.axis_index("vocab")
    row_group, cols = hidden_ref.shape
    rows = row_group * groups
    vocab_dev, width_all = head.shape
    tiles = width_all // LANES
    devices = groups * shards
    me = group * shards + shard
    span = width * LANES

    head_copy = pltpu.make_async_copy(head_hbm, head, local_sem.at[0])
    qkv_copy = pltpu.make_async_copy(qkv_hbm, qkv, local_sem.at[1])
    head_copy.start()
    qkv_copy.start()

    def group_peer(k):
        return (lax.rem(group + k, groups), shard)

    def shard_peer(k):
        return (group, lax.rem(shard + k, shards))

    def send(src, dst, phase, peer):
        pltpu.make_async_remote_copy(
            src_ref=src,
            dst_ref=dst,
            send_sem=send_sem.at[phase],
            recv_sem=recv_sem.at[phase],
            device_id=peer,
            device_id_type=MESH,
        ).start()

    def wait_all(ref, count, sem):
        if count > 0:
            part = ref.at[pl.ds(0, count)]
            pltpu.make_async_copy(part, part, sem).wait()

    barrier = pltpu.get_barrier_semaphore()
    each(1, groups, lambda k: pl.semaphore_signal(barrier, inc=1, device_id=group_peer(k), device_id_type=MESH))
    each(1, shards, lambda k: pl.semaphore_signal(barrier, inc=1, device_id=shard_peer(k), device_id_type=MESH))
    ids[group, 0:1, 0:row_group] = slot_ref[...]
    ids[group, 1:2, 0:row_group] = target_ref[...]
    pl.semaphore_wait(barrier, groups + shards - 2)

    each(1, groups, lambda k: send(ids.at[group], ids.at[group], 0, group_peer(k)))
    each(1, shards, lambda k: send(hidden_ref, pieces.at[shard], 1, shard_peer(k)))
    pieces[shard] = hidden_ref[...]

    wait_all(pieces, shards - 1, recv_sem.at[1])
    for v in range(shards):
        wide_rows[:, v * cols : (v + 1) * cols] = pieces[v].astype(jnp.float32)
    normed[group] = rms_scaled(wide_rows[...], final_gain_ref[...])
    each(1, groups, lambda k: send(normed.at[group], normed.at[group], 2, group_peer(k)))

    wait_all(ids, groups - 1, recv_sem.at[0])
    row_iota = lax.broadcasted_iota(jnp.int32, (rows, row_group), 0)
    lane_iota = lax.broadcasted_iota(jnp.int32, (rows, row_group), 1)
    dealt = jnp.zeros((rows, row_group), jnp.float32)
    owned = jnp.zeros((rows, row_group), jnp.float32)
    for k in range(groups):
        slots = ids[k, 0:1, 0:row_group]
        wanted = ids[k, 1:2, 0:row_group].astype(jnp.float32)
        dealt = dealt + jnp.where(row_iota == slots, wanted, 0.0)
        owned = owned + jnp.where(row_iota == lane_iota + k * row_group, wanted, 0.0)
    offset = me * vocab_dev
    vocab_iota = lax.broadcasted_iota(jnp.int32, (rows, vocab_dev), 1) + offset
    dealt_ids = jnp.sum(dealt, axis=1, keepdims=True).astype(jnp.int32)
    owned_ids = jnp.sum(owned, axis=1, keepdims=True).astype(jnp.int32)
    one_hot = jnp.where(dealt_ids == vocab_iota, 1.0, 0.0).astype(jnp.bfloat16)
    head_copy.wait()
    picked[...] = jnp.dot(one_hot, head[...], preferred_element_type=jnp.float32)
    for k in range(groups):
        picked_out[k] = picked[k * row_group : (k + 1) * row_group, :].astype(jnp.bfloat16)

    def columns(v):
        return pl.ds(pl.multiple_of(lax.div(v * tiles, shards) * LANES, LANES), span)

    def send_piece(k):
        peer = lax.rem(me + k, devices)
        peer_group, peer_shard = lax.div(peer, shards), lax.rem(peer, shards)
        send(picked_out.at[peer_group, :, columns(peer_shard)], picked_in.at[me], 3, (peer_group, peer_shard))

    each(1, devices, send_piece)
    picked_in[me] = picked_out[group, :, columns(shard)]

    wait_all(normed, groups - 1, recv_sem.at[2])
    for k in range(groups):
        rows_all[k * row_group : (k + 1) * row_group, :] = normed[k].astype(jnp.float32)
    logits = lax.dot_general(
        rows_all[...].astype(jnp.bfloat16),
        head[...],
        (((1,), (1,)), ((), ())),
        preferred_element_type=jnp.float32,
    )
    top = jnp.max(logits, axis=1, keepdims=True)
    shifted = logits - top
    expons = jnp.exp(shifted)
    columns_of = (
        top,
        jnp.sum(expons, axis=1, keepdims=True),
        jnp.sum(expons * shifted, axis=1, keepdims=True),
        jnp.sum(jnp.where(owned_ids == vocab_iota, logits, 0.0), axis=1, keepdims=True),
    )
    lanes = stats_one.shape[2]
    diagonal = lax.broadcasted_iota(jnp.int32, (rows, lanes), 0) == lax.broadcasted_iota(
        jnp.int32, (rows, lanes), 1
    )
    put_stats(
        stats_one,
        shard,
        [jnp.sum(jnp.where(diagonal, column, 0.0), axis=0, keepdims=True) for column in columns_of],
    )
    each(1, shards, lambda k: send(stats_one.at[shard], stats_one.at[shard], 4, shard_peer(k)))

    wait_all(picked_in, devices - 1, recv_sem.at[3])
    if devices <= UNROLL_MAX:
        total = jnp.sum(picked_in[...].astype(jnp.float32), axis=0)
    else:
        total = lax.fori_loop(
            0,
            devices,
            lambda k, so_far: so_far + picked_in[k].astype(jnp.float32),
            jnp.zeros((row_group, span), jnp.float32),
        )
    summed[shard] = total.astype(jnp.bfloat16)
    each(1, shards, lambda k: send(summed.at[shard], summed.at[shard], 5, shard_peer(k)))

    wait_all(stats_one, shards - 1, recv_sem.at[4])
    put_stats(stats_two, group, merged(stats_one))
    each(1, groups, lambda k: send(stats_two.at[group], stats_two.at[group], 6, group_peer(k)))

    qkv_copy.wait()
    wait_all(summed, shards - 1, recv_sem.at[5])
    for v in range(shards):
        embedded[:, starts[v] * LANES : starts[v] * LANES + span] = summed[v].astype(jnp.float32)
    first_normed = rms_scaled(embedded[...], first_gain_ref[...])
    out_ref[...] = jnp.dot(first_normed, qkv[...], preferred_element_type=jnp.float32).astype(out_ref.dtype)

    wait_all(stats_two, groups - 1, recv_sem.at[6])
    row_top, row_total, row_weighted, row_target = merged(stats_two)
    log_total = jnp.log(row_total)
    logprob = row_target - row_top - log_total
    entropy = log_total - row_weighted / row_total
    for ref, values in ((logprob_ref, logprob), (entropy_ref, entropy)):
        mine = values[:, 0:row_group]
        for k in range(1, groups):
            mine = jnp.where(group == k, values[:, k * row_group : (k + 1) * row_group], mine)
        ref[...] = mine

    wait_all(ids, groups - 1, send_sem.at[0])
    wait_all(pieces, shards - 1, send_sem.at[1])
    wait_all(normed, groups - 1, send_sem.at[2])
    wait_all(picked_in, devices - 1, send_sem.at[3])
    wait_all(stats_one, shards - 1, send_sem.at[4])
    wait_all(summed, shards - 1, send_sem.at[5])
    wait_all(stats_two, groups - 1, send_sem.at[6])


def local(groups, shards, hidden, dealt_slot, targets, final_gain, vocab_head, first_gain, qkv_weight):
    row_group, cols = hidden.shape
    rows = row_group * groups
    width_all = vocab_head.shape[1]
    tiles = width_all // LANES
    starts = [v * tiles // shards for v in range(shards)]
    width = max(b - a for a, b in zip(starts, starts[1:] + [tiles]))
    span = width * LANES
    lanes = -(-rows // LANES) * LANES
    qkv_cols = qkv_weight.shape[1]
    vmem = pl.BlockSpec(memory_space=pltpu.VMEM)
    hbm = pl.BlockSpec(memory_space=pl.ANY)
    logprob, entropy, projected = pl.pallas_call(
        functools.partial(kernel, groups, shards, starts, width),
        out_shape=(
            jax.ShapeDtypeStruct((1, row_group), jnp.float32),
            jax.ShapeDtypeStruct((1, row_group), jnp.float32),
            jax.ShapeDtypeStruct((row_group, qkv_cols), jnp.bfloat16),
        ),
        in_specs=[vmem, vmem, vmem, vmem, hbm, vmem, hbm],
        out_specs=(vmem, vmem, vmem),
        scratch_shapes=[
            pltpu.VMEM(vocab_head.shape, jnp.bfloat16),
            pltpu.VMEM(qkv_weight.shape, jnp.bfloat16),
            pltpu.VMEM((groups, 8, LANES), jnp.int32),
            pltpu.VMEM((shards, row_group, cols), jnp.bfloat16),
            pltpu.VMEM((row_group, width_all), jnp.float32),
            pltpu.VMEM((groups, row_group, width_all), jnp.bfloat16),
            pltpu.VMEM((rows, width_all), jnp.float32),
            pltpu.VMEM((rows, width_all), jnp.float32),
            pltpu.VMEM((groups, row_group, width_all), jnp.bfloat16),
            pltpu.VMEM((groups * shards, row_group, span), jnp.bfloat16),
            pltpu.VMEM((shards, row_group, span), jnp.bfloat16),
            pltpu.VMEM((row_group, width_all), jnp.float32),
            pltpu.VMEM((shards, 8, lanes), jnp.float32),
            pltpu.VMEM((groups, 8, lanes), jnp.float32),
            pltpu.SemaphoreType.DMA((2,)),
            pltpu.SemaphoreType.DMA((7,)),
            pltpu.SemaphoreType.DMA((7,)),
        ],
        compiler_params=pltpu.CompilerParams(
            collective_id=0, has_side_effects=True, vmem_limit_bytes=48 * 1024 * 1024
        ),
    )(
        hidden,
        dealt_slot.reshape(1, row_group),
        targets.reshape(1, row_group),
        final_gain.reshape(1, width_all),
        vocab_head,
        first_gain.reshape(1, width_all),
        qkv_weight,
    )
    return (logprob.reshape(row_group), entropy.reshape(row_group), projected.T)


def solution(mesh):
    return jax.shard_map(
        functools.partial(local, mesh.shape["group"], mesh.shape["vocab"]),
        mesh=mesh,
        in_specs=(
            P("group", "vocab"),
            P("group"),
            P("group"),
            P(),
            P(("group", "vocab"), None),
            P(),
            P(None, "vocab"),
        ),
        out_specs=(P("group"), P("group"), P("vocab", "group")),
        check_vma=False,
    )
```

time: 168 us -> 31 us (0.18)
  blocking collectives: 117 us -> 0 us
  Pallas kernels: 0 us -> 21.7 us
  between operations: 15.5 us -> 0.65 us
  starting transfers between devices: 10.8 us -> 0 us
  other arithmetic: 7.31 us -> 0 us
  matrix products: 4.37 us -> 0 us
  waiting for transfers between devices: 3.6 us -> 0 us
    unnamed x2 -> x0, blocking collectives: 44.2 us -> none
    all_gather x2 -> x0, blocking collectives: 36.3 us -> none  [the longest x1 31.1 us: local(): dealt_rows = lax.all_gather(dealt_cols, 'vocab', axis=1, tiled=True)]
    psum x1 -> x0, blocking collectives: 36.1 us -> none  [local(): embedded = lax.psum(shared, 'vocab').astype(jnp.float32)]
    pallas_call x0 -> x1, Pallas kernels: none -> 21.7 us  [local(): pl.pallas_call(functools.partial(kernel, groups, shards, starts, width),...]
    all_to_all x3 -> x0, starting transfers between devices: 10.8 us -> none  [the longest x1 4.24 us: local(): lax.all_to_all(send_slots.reshape(groups, quota), 'group', split_axis=0,...]
    dot_general x4 -> x0, matrix products: 4.37 us -> none  [the longest x1 2.55 us: local(): jnp.einsum('rd,dc->cr', first_normed.astype(jnp.float32), weight_wide)]
    all_to_all x3 -> x0, waiting for transfers between devices: 3.59 us -> none  [the longest x1 3.58 us: local(): lax.all_to_all(send_targets.reshape(groups, quota), 'group', split_axis=0...]
    unnamed x21 -> x13, local copies, waits for them, and re-layouts: 4.04 us -> 6.88 us
  transfers between devices with their start and end apart: 4 -> 0, of which waited for: 1 -> 0; matrix products, arithmetic and copies ran while one was open for 8% -> 0% of each run, Pallas kernels for 0% -> 0%
where the time goes in v1:
time: 31 us; the launch traced here: 30.6 us
  Pallas kernels  21.7 us (70%)
  local copies, waits for them, and re-layouts  8.31 us (27%)
  between operations  0.65 us (2%)
    pallas_call x1, Pallas kernels, local(): pl.pallas_call(functools.partial(kernel, groups, shards, starts, width),...  21.7 us
    unnamed x13, local copies, waits for them, and re-layouts  6.88 us
    reshape x1, local copies, waits for them, and re-layouts, local(): final_gain.reshape(1, width_all)  0.72 us
    reshape x1, local copies, waits for them, and re-layouts, local(): first_gain.reshape(1, width_all)  0.71 us

profile of v1, /device:TPU:0, one launch (start us, length us, event | category | flops | bytes accessed | tf_op | source)
XLA Modules:
  0.0 30.6 jit_solution(6171829133423213333)
XLA Ops:
  0.6 0.7 %reshape.26.final_gain_ref = f32[1,2560]{1,0:T(1,128)S(1)} reshape(f32[2560]{0:T(1024)} %param.10) | data formatting | bytes 20480 | tf_op jit(solution)/shard_map/reshape | solution.py:288
  1.3 0.7 %reshape.27.first_gain_ref = f32[1,2560]{1,0:T(1,128)S(1)} reshape(f32[2560]{0:T(1024)} %param.12) | data formatting | bytes 20480 | tf_op jit(solution)/shard_map/reshape | solution.py:290
  2.1 0.0 copy-start
  2.1 1.7 %copy-done = bf16[512,2560]{1,0:T(8,128)(2,1)S(1)} copy-done((bf16[512,2560]{1,0:T(8,128)(2,1)S(1)}, bf16[512,2560]{1,0:T(8,128)(2,1)}, u32[]{:S(2)}) %copy-start) | copy-done | bytes 2621464
  3.8 0.0 copy-start.1
  3.8 1.5 %copy-done.1 = bf16[2560,384]{1,0:T(8,128)(2,1)S(1)} copy-done((bf16[2560,384]{1,0:T(8,128)(2,1)S(1)}, bf16[2560,384]{1,0:T(8,128)(2,1)}, u32[]{:S(2)}) %copy-start.1) | copy-done | bytes 1966104
  5.3 0.0 copy-start.2
  5.3 0.7 %copy-done.2 = bf16[4,320]{1,0:T(4,128)(2,1)S(1)} copy-done((bf16[4,320]{1,0:T(4,128)(2,1)S(1)}, bf16[4,320]{1,0:T(4,128)(2,1)}, u32[]{:S(2)}) %copy-start.2) | copy-done | bytes 2584
  6.0 0.0 copy-start.3
  6.0 0.7 %copy-done.3 = s32[4]{0:T(128)S(1)} copy-done((s32[4]{0:T(128)S(1)}, s32[4]{0:T(128)}, u32[]{:S(2)}) %copy-start.3) | copy-done | bytes 40
  6.7 0.0 copy-start.4
  6.7 0.7 %copy-done.4 = s32[4]{0:T(128)S(1)} copy-done((s32[4]{0:T(128)S(1)}, s32[4]{0:T(128)}, u32[]{:S(2)}) %copy-start.4) | copy-done | bytes 40
  7.3 21.7 %shard_map.94 = (f32[1,4]{1,0:T(1,128)S(1)}, f32[1,4]{1,0:T(1,128)S(1)}, bf16[4,384]{1,0:T(4,128)(2,1)S(1)}) custom-call(bf16[4,320]{1,0:T(4,128)(2,1)S(1)} %copy-done.2, s32[1,4]{1,0:T(1,128)S(1)} %bitcast.6, s32[1,4]{1,0:T(1,128)S(1)} %bitcast.7, f32[1,2560]{1,0:T(1,128)S(1)} %reshape.26.final_gain_ref, bf16[512,2560]{1,0:T(8,128)(2,1)S(1)} %copy-done, ...), custom_call_target="tpu_custom_call" | custom-call | tf_op jit(solution)/shard_map/pallas_call | solution.py:253
  29.0 0.5 %copy.13 = f32[4]{0:T(128)} copy(f32[4]{0:T(128)S(1)} %bitcast.9) | data formatting | bytes 32
  29.6 0.5 %copy.14 = f32[4]{0:T(128)} copy(f32[4]{0:T(128)S(1)} %bitcast.8) | data formatting | bytes 32
  30.1 0.6 %copy.15 = bf16[384,4]{0,1:T(4,128)(2,1)} copy(bf16[384,4]{0,1:T(4,128)(2,1)S(1)} %bitcast.5) | data formatting | bytes 6144
Async XLA Ops:
  2.1 1.7 %copy-start = (bf16[512,2560]{1,0:T(8,128)(2,1)S(1)}, bf16[512,2560]{1,0:T(8,128)(2,1)}, u32[]{:S(2)}) copy-start(bf16[512,2560]{1,0:T(8,128)(2,1)} %head_hbm.1) | copy-start | bytes 7864324
  3.8 1.5 %copy-start.1 = (bf16[2560,384]{1,0:T(8,128)(2,1)S(1)}, bf16[2560,384]{1,0:T(8,128)(2,1)}, u32[]{:S(2)}) copy-start(bf16[2560,384]{1,0:T(8,128)(2,1)} %qkv_hbm.1) | copy-start | bytes 5898244
  5.3 0.7 %copy-start.2 = (bf16[4,320]{1,0:T(4,128)(2,1)S(1)}, bf16[4,320]{1,0:T(4,128)(2,1)}, u32[]{:S(2)}) copy-start(bf16[4,320]{1,0:T(4,128)(2,1)} %hidden_ref.1) | copy-start | bytes 7684
  6.0 0.7 %copy-start.3 = (s32[4]{0:T(128)S(1)}, s32[4]{0:T(128)}, u32[]{:S(2)}) copy-start(s32[4]{0:T(128)} %param.8) | copy-start | bytes 52
  6.7 0.7 %copy-start.4 = (s32[4]{0:T(128)S(1)}, s32[4]{0:T(128)}, u32[]{:S(2)}) copy-start(s32[4]{0:T(128)} %param.9) | copy-start | bytes 52

commit v2 on v1

--- a/solution.py
+++ b/solution.py
@@ -53,18 +53,22 @@
     shards,
     starts,
     width,
-    hidden_ref,
-    slot_ref,
-    target_ref,
-    final_gain_ref,
+    hidden_hbm,
+    slot_hbm,
+    target_hbm,
+    final_gain_hbm,
     head_hbm,
-    first_gain_ref,
+    first_gain_hbm,
     qkv_hbm,
     logprob_ref,
     entropy_ref,
     out_ref,
     head,
     qkv,
+    slot_ref,
+    target_ref,
+    final_gain_ref,
+    first_gain_ref,
     ids,
     pieces,
     wide_rows,
@@ -83,18 +87,13 @@
 ):
     group = lax.axis_index("group")
     shard = lax.axis_index("vocab")
-    row_group, cols = hidden_ref.shape
+    row_group, cols = hidden_hbm.shape
     rows = row_group * groups
     vocab_dev, width_all = head.shape
     tiles = width_all // LANES
     devices = groups * shards
     me = group * shards + shard
     span = width * LANES
-
-    head_copy = pltpu.make_async_copy(head_hbm, head, local_sem.at[0])
-    qkv_copy = pltpu.make_async_copy(qkv_hbm, qkv, local_sem.at[1])
-    head_copy.start()
-    qkv_copy.start()
 
     def group_peer(k):
         return (lax.rem(group + k, groups), shard)
@@ -120,17 +119,29 @@
     barrier = pltpu.get_barrier_semaphore()
     each(1, groups, lambda k: pl.semaphore_signal(barrier, inc=1, device_id=group_peer(k), device_id_type=MESH))
     each(1, shards, lambda k: pl.semaphore_signal(barrier, inc=1, device_id=shard_peer(k), device_id_type=MESH))
+    slot_copy = pltpu.make_async_copy(slot_hbm, slot_ref, local_sem.at[0])
+    target_copy = pltpu.make_async_copy(target_hbm, target_ref, local_sem.at[1])
+    hidden_copy = pltpu.make_async_copy(hidden_hbm, pieces.at[shard], local_sem.at[2])
+    final_copy = pltpu.make_async_copy(final_gain_hbm, final_gain_ref, local_sem.at[3])
+    head_copy = pltpu.make_async_copy(head_hbm, head, local_sem.at[4])
+    first_copy = pltpu.make_async_copy(first_gain_hbm, first_gain_ref, local_sem.at[5])
+    qkv_copy = pltpu.make_async_copy(qkv_hbm, qkv, local_sem.at[6])
+    for copy in (slot_copy, target_copy, hidden_copy, final_copy, head_copy, first_copy, qkv_copy):
+        copy.start()
+    slot_copy.wait()
+    target_copy.wait()
     ids[group, 0:1, 0:row_group] = slot_ref[...]
     ids[group, 1:2, 0:row_group] = target_ref[...]
+    hidden_copy.wait()
     pl.semaphore_wait(barrier, groups + shards - 2)
 
     each(1, groups, lambda k: send(ids.at[group], ids.at[group], 0, group_peer(k)))
-    each(1, shards, lambda k: send(hidden_ref, pieces.at[shard], 1, shard_peer(k)))
-    pieces[shard] = hidden_ref[...]
+    each(1, shards, lambda k: send(pieces.at[shard], pieces.at[shard], 1, shard_peer(k)))
 
     wait_all(pieces, shards - 1, recv_sem.at[1])
     for v in range(shards):
         wide_rows[:, v * cols : (v + 1) * cols] = pieces[v].astype(jnp.float32)
+    final_copy.wait()
     normed[group] = rms_scaled(wide_rows[...], final_gain_ref[...])
     each(1, groups, lambda k: send(normed.at[group], normed.at[group], 2, group_peer(k)))
 
@@ -211,6 +222,7 @@
     put_stats(stats_two, group, merged(stats_one))
     each(1, groups, lambda k: send(stats_two.at[group], stats_two.at[group], 6, group_peer(k)))
 
+    first_copy.wait()
     qkv_copy.wait()
     wait_all(summed, shards - 1, recv_sem.at[5])
     for v in range(shards):
@@ -249,7 +261,7 @@
     lanes = -(-rows // LANES) * LANES
     qkv_cols = qkv_weight.shape[1]
     vmem = pl.BlockSpec(memory_space=pltpu.VMEM)
-    hbm = pl.BlockSpec(memory_space=pl.ANY)
+    hbm = pl.BlockSpec(memory_space=pltpu.HBM)
     logprob, entropy, projected = pl.pallas_call(
         functools.partial(kernel, groups, shards, starts, width),
         out_shape=(
@@ -257,11 +269,15 @@
             jax.ShapeDtypeStruct((1, row_group), jnp.float32),
             jax.ShapeDtypeStruct((row_group, qkv_cols), jnp.bfloat16),
         ),
-        in_specs=[vmem, vmem, vmem, vmem, hbm, vmem, hbm],
+        in_specs=[hbm] * 7,
         out_specs=(vmem, vmem, vmem),
         scratch_shapes=[
             pltpu.VMEM(vocab_head.shape, jnp.bfloat16),
             pltpu.VMEM(qkv_weight.shape, jnp.bfloat16),
+            pltpu.VMEM((1, row_group), jnp.int32),
+            pltpu.VMEM((1, row_group), jnp.int32),
+            pltpu.VMEM((1, width_all), jnp.float32),
+            pltpu.VMEM((1, width_all), jnp.float32),
             pltpu.VMEM((groups, 8, LANES), jnp.int32),
             pltpu.VMEM((shards, row_group, cols), jnp.bfloat16),
             pltpu.VMEM((row_group, width_all), jnp.float32),
@@ -274,12 +290,12 @@
             pltpu.VMEM((row_group, width_all), jnp.float32),
             pltpu.VMEM((shards, 8, lanes), jnp.float32),
             pltpu.VMEM((groups, 8, lanes), jnp.float32),
-            pltpu.SemaphoreType.DMA((2,)),
+            pltpu.SemaphoreType.DMA((7,)),
             pltpu.SemaphoreType.DMA((7,)),
             pltpu.SemaphoreType.DMA((7,)),
         ],
         compiler_params=pltpu.CompilerParams(
-            collective_id=0, has_side_effects=True, vmem_limit_bytes=48 * 1024 * 1024
+            collective_id=0, has_side_effects=True, vmem_limit_bytes=63 * 1024 * 1024
         ),
     )(
         hidden,

time: 31 us -> 28.9 us (0.932)
  local copies, waits for them, and re-layouts: 8.31 us -> 6.13 us
    unnamed x13 -> x3, local copies, waits for them, and re-layouts: 6.88 us -> 3.52 us
    reshape x1, local copies, waits for them, and re-layouts: 0.71 us -> 1.31 us  [local(): first_gain.reshape(1, width_all)]
    reshape x1, local copies, waits for them, and re-layouts: 0.72 us -> 1.3 us  [local(): final_gain.reshape(1, width_all)]
where the time goes in v2:
time: 28.9 us; the launch traced here: 28.6 us
  Pallas kernels  21.8 us (75%)
  local copies, waits for them, and re-layouts  6.13 us (21%)
  between operations  0.64 us (2%)
    pallas_call x1, Pallas kernels, local(): pl.pallas_call(functools.partial(kernel, groups, shards, starts, width),...  21.8 us
    unnamed x3, local copies, waits for them, and re-layouts  3.52 us
    reshape x1, local copies, waits for them, and re-layouts, local(): first_gain.reshape(1, width_all)  1.31 us
    reshape x1, local copies, waits for them, and re-layouts, local(): final_gain.reshape(1, width_all)  1.3 us

profile of v2, /device:TPU:0, one launch (start us, length us, event | category | flops | bytes accessed | tf_op | source)
XLA Modules:
  0.0 28.6 jit_solution(1575783105200109242)
XLA Ops:
  0.6 1.3 %reshape.26.final_gain_hbm = f32[1,2560]{1,0:T(1,128)} reshape(f32[2560]{0:T(1024)} %param.10) | data formatting | bytes 20480 | tf_op jit(solution)/shard_map/reshape | solution.py:304
  1.9 1.3 %reshape.27.first_gain_hbm = f32[1,2560]{1,0:T(1,128)} reshape(f32[2560]{0:T(1024)} %param.12) | data formatting | bytes 20480 | tf_op jit(solution)/shard_map/reshape | solution.py:306
  3.2 21.8 %shard_map.94 = (f32[1,4]{1,0:T(1,128)}, f32[1,4]{1,0:T(1,128)}, bf16[4,384]{1,0:T(4,128)(2,1)}) custom-call(bf16[4,320]{1,0:T(4,128)(2,1)} %hidden_hbm.1, s32[1,4]{1,0:T(1,128)} %bitcast.6, s32[1,4]{1,0:T(1,128)} %bitcast.7, f32[1,2560]{1,0:T(1,128)} %reshape.26.final_gain_hbm, bf16[512,2560]{1,0:T(8,128)(2,1)} %head_hbm.1, ...), custom_call_target="tpu_custom_call" | custom-call | tf_op jit(solution)/shard_map/pallas_call | solution.py:265
  25.0 1.1 %copy.13 = f32[4]{0:T(128)} copy(f32[4]{0:T(128)} %bitcast.9) | data formatting | bytes 32
  26.2 1.1 %copy.14 = f32[4]{0:T(128)} copy(f32[4]{0:T(128)} %bitcast.8) | data formatting | bytes 32
  27.3 1.3 %copy.15 = bf16[384,4]{0,1:T(4,128)(2,1)} copy(bf16[384,4]{0,1:T(4,128)(2,1)} %bitcast.5) | data formatting | bytes 6144

commit v3 on v2

--- a/solution.py
+++ b/solution.py
@@ -122,9 +122,9 @@
     slot_copy = pltpu.make_async_copy(slot_hbm, slot_ref, local_sem.at[0])
     target_copy = pltpu.make_async_copy(target_hbm, target_ref, local_sem.at[1])
     hidden_copy = pltpu.make_async_copy(hidden_hbm, pieces.at[shard], local_sem.at[2])
-    final_copy = pltpu.make_async_copy(final_gain_hbm, final_gain_ref, local_sem.at[3])
+    final_copy = pltpu.make_async_copy(final_gain_hbm, final_gain_ref.at[0], local_sem.at[3])
     head_copy = pltpu.make_async_copy(head_hbm, head, local_sem.at[4])
-    first_copy = pltpu.make_async_copy(first_gain_hbm, first_gain_ref, local_sem.at[5])
+    first_copy = pltpu.make_async_copy(first_gain_hbm, first_gain_ref.at[0], local_sem.at[5])
     qkv_copy = pltpu.make_async_copy(qkv_hbm, qkv, local_sem.at[6])
     for copy in (slot_copy, target_copy, hidden_copy, final_copy, head_copy, first_copy, qkv_copy):
         copy.start()
@@ -137,13 +137,6 @@
 
     each(1, groups, lambda k: send(ids.at[group], ids.at[group], 0, group_peer(k)))
     each(1, shards, lambda k: send(pieces.at[shard], pieces.at[shard], 1, shard_peer(k)))
-
-    wait_all(pieces, shards - 1, recv_sem.at[1])
-    for v in range(shards):
-        wide_rows[:, v * cols : (v + 1) * cols] = pieces[v].astype(jnp.float32)
-    final_copy.wait()
-    normed[group] = rms_scaled(wide_rows[...], final_gain_ref[...])
-    each(1, groups, lambda k: send(normed.at[group], normed.at[group], 2, group_peer(k)))
 
     wait_all(ids, groups - 1, recv_sem.at[0])
     row_iota = lax.broadcasted_iota(jnp.int32, (rows, row_group), 0)
@@ -176,6 +169,13 @@
     each(1, devices, send_piece)
     picked_in[me] = picked_out[group, :, columns(shard)]
 
+    wait_all(pieces, shards - 1, recv_sem.at[1])
+    for v in range(shards):
+        wide_rows[:, v * cols : (v + 1) * cols] = pieces[v].astype(jnp.float32)
+    final_copy.wait()
+    normed[group] = rms_scaled(wide_rows[...], final_gain_ref[...])
+    each(1, groups, lambda k: send(normed.at[group], normed.at[group], 2, group_peer(k)))
+
     wait_all(normed, groups - 1, recv_sem.at[2])
     for k in range(groups):
         rows_all[k * row_group : (k + 1) * row_group, :] = normed[k].astype(jnp.float32)
@@ -248,6 +248,15 @@
     wait_all(stats_one, shards - 1, send_sem.at[4])
     wait_all(summed, shards - 1, send_sem.at[5])
     wait_all(stats_two, groups - 1, send_sem.at[6])
+
+
+def hand_over(*refs):
+    sems = refs[-1]
+    copies = [pltpu.make_async_copy(refs[k], refs[k + 3], sems.at[k]) for k in range(3)]
+    for copy in copies:
+        copy.start()
+    for copy in copies:
+        copy.wait()
 
 
 def local(groups, shards, hidden, dealt_slot, targets, final_gain, vocab_head, first_gain, qkv_weight):
@@ -301,12 +310,20 @@
         hidden,
         dealt_slot.reshape(1, row_group),
         targets.reshape(1, row_group),
-        final_gain.reshape(1, width_all),
+        final_gain,
         vocab_head,
-        first_gain.reshape(1, width_all),
+        first_gain,
         qkv_weight,
     )
-    return (logprob.reshape(row_group), entropy.reshape(row_group), projected.T)
+    results = (logprob.reshape(row_group), entropy.reshape(row_group), projected)
+    logprob, entropy, projected = pl.pallas_call(
+        hand_over,
+        out_shape=tuple(jax.ShapeDtypeStruct(r.shape, r.dtype) for r in results),
+        in_specs=[hbm] * 3,
+        out_specs=(hbm,) * 3,
+        scratch_shapes=[pltpu.SemaphoreType.DMA((3,))],
+    )(*results)
+    return (logprob, entropy, projected.T)
 
 
 def solution(mesh):

time: 28.9 us -> 23.9 us (0.83)
  local copies, waits for them, and re-layouts: 6.13 us -> 0 us
  Pallas kernels: 21.8 us -> 23.1 us
    unnamed x3 -> x0, local copies, waits for them, and re-layouts: 3.52 us -> none
    reshape x2 -> x0, local copies, waits for them, and re-layouts: 2.61 us -> none  [the longest x1 1.31 us: local(): first_gain.reshape(1, width_all)]
    pallas_call x0 -> x1, Pallas kernels: none -> 1.25 us  [local(): pl.pallas_call(hand_over, out_shape=tuple((jax.ShapeDtypeStruct(r.shape,...]
where the time goes in v3:
time: 23.9 us; the launch traced here: 23.8 us
  Pallas kernels  23.1 us (97%)
  between operations  0.64 us (3%)
    pallas_call x1, Pallas kernels, local(): pl.pallas_call(functools.partial(kernel, groups, shards, starts, width),...  21.9 us
    pallas_call x1, Pallas kernels, local(): pl.pallas_call(hand_over, out_shape=tuple((jax.ShapeDtypeStruct(r.shape,...  1.25 us

profile of v3, /device:TPU:0, one launch (start us, length us, event | category | flops | bytes accessed | tf_op | source)
XLA Modules:
  0.0 23.8 jit_solution(10294991122339957287)
XLA Ops:
  0.6 21.9 %shard_map.94 = (f32[1,4]{1,0:T(1,128)}, f32[1,4]{1,0:T(1,128)}, bf16[4,384]{1,0:T(4,128)(2,1)}) custom-call(bf16[4,320]{1,0:T(4,128)(2,1)} %hidden_hbm.1, s32[1,4]{1,0:T(1,128)} %bitcast.7, s32[1,4]{1,0:T(1,128)} %bitcast.8, f32[2560]{0:T(1024)} %final_gain_hbm.1, bf16[512,2560]{1,0:T(8,128)(2,1)} %head_hbm.1, f32[2560]{0:T(1024)} %first_gain_hbm.1, ...), custom_call_target="tpu_custom_call" | custom-call | tf_op jit(solution)/shard_map/pallas_call | solution.py:274
  22.5 1.3 %shard_map.95 = (f32[4]{0:T(128)}, f32[4]{0:T(128)}, bf16[4,384]{1,0:T(4,128)(2,1)}) custom-call(f32[4]{0:T(128)} %bitcast.5, f32[4]{0:T(128)} %bitcast.6, bf16[4,384]{1,0:T(4,128)(2,1)} %get-tuple-element.11.refs_2_), custom_call_target="tpu_custom_call" | custom-call | tf_op jit(solution)/shard_map/pallas_call | solution.py:319

commit v4 on v3

--- a/solution.py
+++ b/solution.py
@@ -71,16 +71,13 @@
     first_gain_ref,
     ids,
     pieces,
-    wide_rows,
-    normed,
     rows_all,
     picked,
     picked_out,
     picked_in,
     summed,
     embedded,
-    stats_one,
-    stats_two,
+    stats,
     local_sem,
     send_sem,
     recv_sem,
@@ -98,6 +95,10 @@
     def group_peer(k):
         return (lax.rem(group + k, groups), shard)
 
+    def any_peer(k):
+        peer = lax.rem(me + k, devices)
+        return (lax.div(peer, shards), lax.rem(peer, shards))
+
     def shard_peer(k):
         return (group, lax.rem(shard + k, shards))
 
@@ -117,11 +118,10 @@
             pltpu.make_async_copy(part, part, sem).wait()
 
     barrier = pltpu.get_barrier_semaphore()
-    each(1, groups, lambda k: pl.semaphore_signal(barrier, inc=1, device_id=group_peer(k), device_id_type=MESH))
-    each(1, shards, lambda k: pl.semaphore_signal(barrier, inc=1, device_id=shard_peer(k), device_id_type=MESH))
+    each(1, devices, lambda k: pl.semaphore_signal(barrier, inc=1, device_id=any_peer(k), device_id_type=MESH))
     slot_copy = pltpu.make_async_copy(slot_hbm, slot_ref, local_sem.at[0])
     target_copy = pltpu.make_async_copy(target_hbm, target_ref, local_sem.at[1])
-    hidden_copy = pltpu.make_async_copy(hidden_hbm, pieces.at[shard], local_sem.at[2])
+    hidden_copy = pltpu.make_async_copy(hidden_hbm, pieces.at[me], local_sem.at[2])
     final_copy = pltpu.make_async_copy(final_gain_hbm, final_gain_ref.at[0], local_sem.at[3])
     head_copy = pltpu.make_async_copy(head_hbm, head, local_sem.at[4])
     first_copy = pltpu.make_async_copy(first_gain_hbm, first_gain_ref.at[0], local_sem.at[5])
@@ -133,10 +133,10 @@
     ids[group, 0:1, 0:row_group] = slot_ref[...]
     ids[group, 1:2, 0:row_group] = target_ref[...]
     hidden_copy.wait()
-    pl.semaphore_wait(barrier, groups + shards - 2)
+    pl.semaphore_wait(barrier, devices - 1)
 
     each(1, groups, lambda k: send(ids.at[group], ids.at[group], 0, group_peer(k)))
-    each(1, shards, lambda k: send(pieces.at[shard], pieces.at[shard], 1, shard_peer(k)))
+    each(1, devices, lambda k: send(pieces.at[me], pieces.at[me], 1, any_peer(k)))
 
     wait_all(ids, groups - 1, recv_sem.at[0])
     row_iota = lax.broadcasted_iota(jnp.int32, (rows, row_group), 0)
@@ -169,18 +169,17 @@
     each(1, devices, send_piece)
     picked_in[me] = picked_out[group, :, columns(shard)]
 
-    wait_all(pieces, shards - 1, recv_sem.at[1])
-    for v in range(shards):
-        wide_rows[:, v * cols : (v + 1) * cols] = pieces[v].astype(jnp.float32)
+    wait_all(pieces, devices - 1, recv_sem.at[1])
+    for k in range(groups):
+        for v in range(shards):
+            rows_all[k * row_group : (k + 1) * row_group, v * cols : (v + 1) * cols] = pieces[
+                k * shards + v
+            ].astype(jnp.float32)
     final_copy.wait()
-    normed[group] = rms_scaled(wide_rows[...], final_gain_ref[...])
-    each(1, groups, lambda k: send(normed.at[group], normed.at[group], 2, group_peer(k)))
-
-    wait_all(normed, groups - 1, recv_sem.at[2])
-    for k in range(groups):
-        rows_all[k * row_group : (k + 1) * row_group, :] = normed[k].astype(jnp.float32)
+    normed = rms_scaled(rows_all[...], final_gain_ref[...])
+
     logits = lax.dot_general(
-        rows_all[...].astype(jnp.bfloat16),
+        normed,
         head[...],
         (((1,), (1,)), ((), ())),
         preferred_element_type=jnp.float32,
@@ -194,16 +193,16 @@
         jnp.sum(expons * shifted, axis=1, keepdims=True),
         jnp.sum(jnp.where(owned_ids == vocab_iota, logits, 0.0), axis=1, keepdims=True),
     )
-    lanes = stats_one.shape[2]
+    lanes = stats.shape[2]
     diagonal = lax.broadcasted_iota(jnp.int32, (rows, lanes), 0) == lax.broadcasted_iota(
         jnp.int32, (rows, lanes), 1
     )
     put_stats(
-        stats_one,
-        shard,
+        stats,
+        me,
         [jnp.sum(jnp.where(diagonal, column, 0.0), axis=0, keepdims=True) for column in columns_of],
     )
-    each(1, shards, lambda k: send(stats_one.at[shard], stats_one.at[shard], 4, shard_peer(k)))
+    each(1, devices, lambda k: send(stats.at[me], stats.at[me], 2, any_peer(k)))
 
     wait_all(picked_in, devices - 1, recv_sem.at[3])
     if devices <= UNROLL_MAX:
@@ -216,22 +215,19 @@
             jnp.zeros((row_group, span), jnp.float32),
         )
     summed[shard] = total.astype(jnp.bfloat16)
-    each(1, shards, lambda k: send(summed.at[shard], summed.at[shard], 5, shard_peer(k)))
-
-    wait_all(stats_one, shards - 1, recv_sem.at[4])
-    put_stats(stats_two, group, merged(stats_one))
-    each(1, groups, lambda k: send(stats_two.at[group], stats_two.at[group], 6, group_peer(k)))
+    each(1, shards, lambda k: send(summed.at[shard], summed.at[shard], 4, shard_peer(k)))
+
 
     first_copy.wait()
     qkv_copy.wait()
-    wait_all(summed, shards - 1, recv_sem.at[5])
+    wait_all(summed, shards - 1, recv_sem.at[4])
     for v in range(shards):
         embedded[:, starts[v] * LANES : starts[v] * LANES + span] = summed[v].astype(jnp.float32)
     first_normed = rms_scaled(embedded[...], first_gain_ref[...])
     out_ref[...] = jnp.dot(first_normed, qkv[...], preferred_element_type=jnp.float32).astype(out_ref.dtype)
 
-    wait_all(stats_two, groups - 1, recv_sem.at[6])
-    row_top, row_total, row_weighted, row_target = merged(stats_two)
+    wait_all(stats, devices - 1, recv_sem.at[2])
+    row_top, row_total, row_weighted, row_target = merged(stats)
     log_total = jnp.log(row_total)
     logprob = row_target - row_top - log_total
     entropy = log_total - row_weighted / row_total
@@ -242,12 +238,10 @@
         ref[...] = mine
 
     wait_all(ids, groups - 1, send_sem.at[0])
-    wait_all(pieces, shards - 1, send_sem.at[1])
-    wait_all(normed, groups - 1, send_sem.at[2])
+    wait_all(pieces, devices - 1, send_sem.at[1])
     wait_all(picked_in, devices - 1, send_sem.at[3])
-    wait_all(stats_one, shards - 1, send_sem.at[4])
-    wait_all(summed, shards - 1, send_sem.at[5])
-    wait_all(stats_two, groups - 1, send_sem.at[6])
+    wait_all(stats, devices - 1, send_sem.at[2])
+    wait_all(summed, shards - 1, send_sem.at[4])
 
 
 def hand_over(*refs):
@@ -274,9 +268,9 @@
     logprob, entropy, projected = pl.pallas_call(
         functools.partial(kernel, groups, shards, starts, width),
         out_shape=(
-            jax.ShapeDtypeStruct((1, row_group), jnp.float32),
-            jax.ShapeDtypeStruct((1, row_group), jnp.float32),
-            jax.ShapeDtypeStruct((row_group, qkv_cols), jnp.bfloat16),
+            pltpu.VMEM((1, row_group), jnp.float32),
+            pltpu.VMEM((1, row_group), jnp.float32),
+            pltpu.VMEM((row_group, qkv_cols), jnp.bfloat16),
         ),
         in_specs=[hbm] * 7,
         out_specs=(vmem, vmem, vmem),
@@ -288,20 +282,17 @@
             pltpu.VMEM((1, width_all), jnp.float32),
             pltpu.VMEM((1, width_all), jnp.float32),
             pltpu.VMEM((groups, 8, LANES), jnp.int32),
-            pltpu.VMEM((shards, row_group, cols), jnp.bfloat16),
-            pltpu.VMEM((row_group, width_all), jnp.float32),
-            pltpu.VMEM((groups, row_group, width_all), jnp.bfloat16),
+            pltpu.VMEM((groups * shards, row_group, cols), jnp.bfloat16),
             pltpu.VMEM((rows, width_all), jnp.float32),
             pltpu.VMEM((rows, width_all), jnp.float32),
             pltpu.VMEM((groups, row_group, width_all), jnp.bfloat16),
             pltpu.VMEM((groups * shards, row_group, span), jnp.bfloat16),
             pltpu.VMEM((shards, row_group, span), jnp.bfloat16),
             pltpu.VMEM((row_group, width_all), jnp.float32),
-            pltpu.VMEM((shards, 8, lanes), jnp.float32),
-            pltpu.VMEM((groups, 8, lanes), jnp.float32),
+            pltpu.VMEM((groups * shards, 4, lanes), jnp.float32),
             pltpu.SemaphoreType.DMA((7,)),
-            pltpu.SemaphoreType.DMA((7,)),
-            pltpu.SemaphoreType.DMA((7,)),
+            pltpu.SemaphoreType.DMA((5,)),
+            pltpu.SemaphoreType.DMA((5,)),
         ],
         compiler_params=pltpu.CompilerParams(
             collective_id=0, has_side_effects=True, vmem_limit_bytes=63 * 1024 * 1024
@@ -315,15 +306,15 @@
         first_gain,
         qkv_weight,
     )
-    results = (logprob.reshape(row_group), entropy.reshape(row_group), projected)
+    results = [pltpu.with_memory_space_constraint(r, pltpu.VMEM) for r in (logprob, entropy, projected)]
     logprob, entropy, projected = pl.pallas_call(
         hand_over,
         out_shape=tuple(jax.ShapeDtypeStruct(r.shape, r.dtype) for r in results),
-        in_specs=[hbm] * 3,
+        in_specs=[pl.BlockSpec(memory_space=pltpu.VMEM)] * 3,
         out_specs=(hbm,) * 3,
         scratch_shapes=[pltpu.SemaphoreType.DMA((3,))],
     )(*results)
-    return (logprob, entropy, projected.T)
+    return (logprob.reshape(row_group), entropy.reshape(row_group), projected.T)
 
 
 def solution(mesh):

time: 23.9 us -> 22.2 us (0.929)
  Pallas kernels: 23.1 us -> 21.4 us
    pallas_call x1, Pallas kernels: 21.9 us -> 20.8 us  [local(): pl.pallas_call(functools.partial(kernel, groups, shards, starts, width),...]
    pallas_call x1, Pallas kernels: 1.25 us -> 0.61 us  [local(): pl.pallas_call(hand_over, out_shape=tuple((jax.ShapeDtypeStruct(r.shape,...]
where the time goes in v4:
time: 22.2 us; the launch traced here: 22 us
  Pallas kernels  21.4 us (96%)
  between operations  0.64 us (3%)
    pallas_call x1, Pallas kernels, local(): pl.pallas_call(functools.partial(kernel, groups, shards, starts, width),...  20.8 us
    pallas_call x1, Pallas kernels, local(): pl.pallas_call(hand_over, out_shape=tuple((jax.ShapeDtypeStruct(r.shape,...  0.61 us

profile of v4, /device:TPU:0, one launch (start us, length us, event | category | flops | bytes accessed | tf_op | source)
XLA Modules:
  0.0 22.0 jit_solution(10814496854394468541)
XLA Ops:
  0.6 20.8 %shard_map.94 = (f32[1,4]{1,0:T(1,128)S(1)}, f32[1,4]{1,0:T(1,128)S(1)}, bf16[4,384]{1,0:T(4,128)(2,1)S(1)}) custom-call(bf16[4,320]{1,0:T(4,128)(2,1)} %hidden_hbm.1, s32[1,4]{1,0:T(1,128)} %bitcast.5, s32[1,4]{1,0:T(1,128)} %bitcast.6, f32[2560]{0:T(1024)} %final_gain_hbm.1, bf16[512,2560]{1,0:T(8,128)(2,1)} %head_hbm.1, f32[2560]{0:T(1024)} %first_gain_hbm.1, ...), custom_call_target="tpu_custom_call" | custom-call | tf_op jit(solution)/shard_map/pallas_call | solution.py:268
  21.4 0.6 %shard_map.95 = (f32[1,4]{1,0:T(1,128)}, f32[1,4]{1,0:T(1,128)}, bf16[4,384]{1,0:T(4,128)(2,1)}) custom-call(f32[1,4]{1,0:T(1,128)S(1)} %get-tuple-element.9.refs_0_, f32[1,4]{1,0:T(1,128)S(1)} %get-tuple-element.10.refs_1_, bf16[4,384]{1,0:T(4,128)(2,1)S(1)} %get-tuple-element.11.refs_2_), custom_call_target="tpu_custom_call" | custom-call | tf_op jit(solution)/shard_map/pallas_call | solution.py:310
